TPU v7x, 128 devices: a whole 4x4x4 slice. The times are simulated.
128 devices in a mesh: pipe: 2 (over core), dp: 16 (over z, y), tensor: 4 (over x).
Axes of the slice: x: 4, y: 4, z: 4, core: 2. Of those that a mesh axis runs over, the one named last changes fastest.
Arguments:
- boundary: bfloat16 [2, 2, 16, 128, 768], P('pipe', None, 'dp'), may hold values from -6 to 6
- norm_gains: bfloat16 [2, 4, 768], P('pipe', None, 'dp'), may hold values from 0.25 to 1.75
- attn_qkv: bfloat16 [2, 2, 3, 768, 768], P('pipe', None, None, 'dp', 'tensor'), may hold values from -0.21875 to 0.21875
- attn_out: bfloat16 [2, 2, 768, 768], P('pipe', None, 'tensor', 'dp'), may hold values from -0.875 to 0.875
- mlp_in: bfloat16 [2, 768, 3072], P('pipe', 'dp', 'tensor'), may hold values from -0.21875 to 0.21875
- mlp_out: bfloat16 [2, 3072, 768], P('pipe', 'tensor', 'dp'), may hold values from -0.109375 to 0.109375
- expert_in: bfloat16 [2, 16, 768, 3072], P('pipe', 'dp', None, 'tensor'), may hold values from -0.21875 to 0.21875
- expert_out: bfloat16 [2, 16, 3072, 768], P('pipe', 'dp', 'tensor'), may hold values from -0.109375 to 0.109375
- expert_ids: int32 [2, 2, 16, 128, 2], P('pipe', None, 'dp'), may hold values from 0 to 15, as said below
- expert_slots: int32 [2, 2, 16, 128, 2], P('pipe', None, 'dp'), may hold values from 0 to 19, as said below
- gate_weights: float32 [2, 2, 16, 128, 2], P('pipe', None, 'dp'), may hold values from 0.25 to 0.75
Outputs:
- section_results: float32 [2, 2, 16, 128, 768], P('pipe', None, 'dp')
- norm_gains_grad: float32 [2, 4, 768], P('pipe', None, 'dp')
- attn_qkv_grad: float32 [2, 2, 3, 768, 768], P('pipe', None, None, 'dp', 'tensor')
- attn_out_grad: float32 [2, 2, 768, 768], P('pipe', None, 'tensor', 'dp')
- mlp_in_grad: float32 [2, 768, 3072], P('pipe', 'dp', 'tensor')
- mlp_out_grad: float32 [2, 3072, 768], P('pipe', 'tensor', 'dp')
- expert_in_grad: float32 [2, 16, 768, 3072], P('pipe', 'dp', None, 'tensor')
- expert_out_grad: float32 [2, 16, 3072, 768], P('pipe', 'dp', 'tensor')
Inputs may be any that keep to these rules, and one draw needn't show every extreme that they name: `expert_ids`: in each section and micro-batch, each of the 128 tokens of one index of dp names two different experts, and no expert is named more than 20 times by them; in each section and micro-batch some expert is named exactly 20 times by the tokens of every index of dp. `expert_slots`: within the tokens of one index of dp in one section and micro-batch, the slots given for one expert are all different.
All inputs are finite; a program needn't handle non-finite values.
Results may differ from a plain program's by a relative error of at most 0.039.
Values may be sent and summed in bfloat16 or wider, within the bound.
A program may use at most 192 MiB of HBM per device.

v0:
```python
import functools

import jax
import jax.numpy as jnp
from jax import lax
from jax.experimental import pallas as pl
from jax.experimental.pallas import tpu as pltpu
from jax.sharding import PartitionSpec as P

MESH = pl.DeviceIdType.MESH
BF16 = jnp.bfloat16
F32 = jnp.float32
HEAD_DIM = 64
EPSILON = 1e-06
CAP = 20
MAIN = 16
MICRO = 2


def dims(lhs, rhs, left_dim, right_dim):
    return lax.dot_general(
        lhs, rhs, (((left_dim,), (right_dim,)), ((), ())), preferred_element_type=F32
    )


def nn(lhs, rhs):
    return dims(lhs, rhs, 1, 0)


def nt(lhs, rhs):
    return dims(lhs, rhs, 1, 1)


def tn(lhs, rhs):
    return dims(lhs, rhs, 0, 0)


def normal_cdf(pre):
    return 0.5 * (1.0 + lax.erf(pre * 0.7071067811865476))


def gelu_slope(pre, phi):
    return phi + pre * (0.3989422804014327 * jnp.exp(-0.5 * pre * pre))


def kernel(
    nx,
    nd,
    bnd,
    ids,
    seat,
    gate,
    sq,
    so,
    mi,
    mo,
    gains,
    ein,
    eout,
    res,
    dense_sum,
    feed_sum,
    gains_sum,
    ei_own,
    eo_own,
    ei_far,
    eo_far,
    ra,
    rm,
    rg,
    rt_in,
    sg,
    sa,
    sm,
    put,
    xh,
    wa,
    wm,
    we,
    wg,
    gn,
    rt,
    gt,
    bx,
    sel,
    sel_back,
    pk,
    hs,
    ags,
    rs_out,
    rs_in,
    a2_out,
    a2_in,
    proj,
    mix,
    prb,
    dgm,
    act,
    arr,
    dge,
    ace,
    ga,
    gm,
    pa,
    pm,
    eg,
    dgn,
    gx,
    gs,
    cur,
    hout,
    gout,
    ag_send,
    ag_recv,
    rs_send,
    rs_recv,
    a2_send,
    a2_recv,
    w_send,
    w_recv,
    w_own,
    wf_send,
    wf_recv,
    m_send,
    m_recv,
    m_own,
    pg_send,
    pg_recv,
    ch_send,
    ch_recv,
    ch_own,
    e_send,
    e_recv,
    e_own,
    res_send,
    res_recv,
    res_own,
    gx_send,
    gx_recv,
    rg_send,
    rg_recv,
    rg_own,
):
    core = lax.axis_index("pipe")
    md = lax.axis_index("dp")
    mx = lax.axis_index("tensor")
    other = 1 - core
    rows, features = cur.shape
    tokens = nx * rows
    shard_rows = sa.shape[1]
    wide_features = sq.shape[3]
    heads = wide_features // HEAD_DIM
    quarters = features // 256
    slots = nd * CAP
    extras = CAP - MAIN

    def x_peer(step):
        peer = mx + step
        return peer - jnp.where(peer >= nx, nx, 0)

    x_steps = sorted(range(1, nx), key=lambda step: -min(step, nx - step))

    def d_peer(step):
        peer = md + step
        return peer - jnp.where(peer >= nd, nd, 0)

    unit = 5 if (nd - 1) % 5 == 0 else 1

    def each_step(push):
        def some_steps(turn, carry):
            for at in range(unit):
                push(1 + turn * unit + at)
            return carry

        lax.fori_loop(0, (nd - 1) // unit, some_steps, 0)

    def far_first(step):
        turned = step + nd // 2 - 1
        return jnp.where(turned >= nd, turned - nd + 1, turned)

    def remote(src, dst, send, recv, **where):
        return pltpu.make_async_remote_copy(
            src_ref=src,
            dst_ref=dst,
            send_sem=send,
            recv_sem=recv,
            device_id=where,
            device_id_type=MESH,
        )

    def local(src, dst, sem):
        return pltpu.make_async_copy(src, dst, sem)

    def wait_for(ref, sem):
        pltpu.make_async_copy(ref, ref, sem).wait()

    barrier = pltpu.get_barrier_semaphore()

    def greet(step, carry):
        pl.semaphore_signal(
            barrier, inc=1, device_id={"dp": d_peer(step)}, device_id_type=MESH
        )
        return carry

    lax.fori_loop(1, nd, greet, 0)
    for step in range(1, nx):
        pl.semaphore_signal(
            barrier, inc=1, device_id={"tensor": x_peer(step)}, device_id_type=MESH
        )
    for step in range(nx):
        pl.semaphore_signal(
            barrier,
            inc=1,
            device_id={"pipe": other, "tensor": x_peer(step)},
            device_id_type=MESH,
        )

    mine = pl.ds(md * shard_rows, shard_rows)
    shard_src = (sg, sa.at[0], sm, sa.at[1])
    shard_dst = (
        wg.at[core, mine],
        wa.at[core, 0, mine],
        wm.at[core, :, mine],
        wa.at[core, 1, mine],
    )

    def share_weight(which):
        def push(step):
            remote(
                shard_src[which],
                shard_dst[which],
                w_send.at[which],
                w_recv.at[which],
                dp=d_peer(step),
            ).start()

        local(shard_src[which], shard_dst[which], w_own.at[which]).start()
        each_step(push)

    all_but_one = pl.ds(0, (nd - 1) * shard_rows)

    def arrived_part(which):
        if which == 0:
            return wg.at[0, all_but_one]
        if which == 2:
            return wm.at[0, :, all_but_one]
        return wa.at[0, which // 2, all_but_one]

    def whole_part(which, section):
        if which == 0:
            return wg.at[section]
        if which == 2:
            return wm.at[section]
        return wa.at[section, which // 2]

    def weight_forward(which):
        wait_for(arrived_part(which), w_recv.at[which])
        local(shard_src[which], shard_dst[which], w_own.at[which]).wait()
        remote(
            whole_part(which, core),
            whole_part(which, core),
            wf_send.at[which],
            wf_recv.at[which],
            pipe=other,
        ).start()

    def weight_ready(which):
        wait_for(whole_part(which, 0), wf_recv.at[which])

    def misc_copies():
        return (
            remote(bnd.at[other], bx, m_send.at[0], m_recv.at[0], pipe=other),
            remote(rt_in.at[other], rt.at[core], m_send.at[1], m_recv.at[1], pipe=other),
        )

    def expert_copies():
        return (
            remote(ein, we.at[core, 0], m_send.at[2], m_recv.at[2], pipe=other),
            remote(eout, we.at[core, 1], m_send.at[3], m_recv.at[3], pipe=other),
        )

    def expert_own():
        return (
            local(ein, we.at[core, 0], m_own.at[0]),
            local(eout, we.at[core, 1], m_own.at[1]),
        )

    put_row = lax.broadcasted_iota(jnp.int32, put.shape[1:], 0)
    put_col = lax.broadcasted_iota(jnp.int32, put.shape[1:], 1)
    for c in range(4):
        put[c] = jnp.where(put_col == put_row + c * wide_features, 1.0, 0.0).astype(BF16)

    def attention_shard(j):
        total = nn(so[j], put[0])
        for c in range(3):
            total = total + nn(sq[j, c], put[1 + c])
        sa[j] = total.astype(BF16)

    attention_shard(0)
    count = gains.shape[0]
    pick_row = lax.broadcasted_iota(jnp.int32, (count, 128), 0)
    pick_col = lax.broadcasted_iota(jnp.int32, (count, 128), 1)
    sg[...] = tn(gains[...], jnp.where(pick_row == pick_col, 1.0, 0.0).astype(BF16)).astype(BF16)
    for m in range(MICRO):
        expert = ids[m]
        seats = seat[m]
        place = jnp.where(
            seats < MAIN,
            expert * MAIN + seats,
            nd * MAIN + expert * extras + seats - MAIN,
        )
        rt_in[m] = jnp.concatenate(
            [place.astype(F32), gate[m], jnp.zeros((4, tokens), F32)], axis=0
        )

    pl.semaphore_wait(barrier, (nd - 1) + (nx - 1) + nx)

    @pl.when(core == 0)
    def first_attention():
        share_weight(1)

    for copy in misc_copies():
        copy.start()
    share_weight(0)
    sm[0] = mi[...]
    sm[1] = mo[...]
    attention_shard(1)

    @pl.when(core == 0)
    def first_section():
        share_weight(2)
        share_weight(3)

    rt[core] = rt_in[core]
    row_id = lax.broadcasted_iota(jnp.int32, (nd * 16, nd * extras), 0)
    col_id = lax.broadcasted_iota(jnp.int32, (nd * 16, nd * extras), 1)
    back_row = lax.broadcasted_iota(jnp.int32, (nd * extras, nd * 16), 0)
    back_col = lax.broadcasted_iota(jnp.int32, (nd * extras, nd * 16), 1)
    for q in range(quarters):
        hit = (
            ((row_id >> 4) == (col_id >> 2))
            & (((row_id >> 2) & 3) == q)
            & ((row_id & 3) == (col_id & 3))
        )
        sel[q] = jnp.where(hit, 1.0, 0.0).astype(BF16)
        hit = (
            ((back_col >> 4) == (back_row >> 2))
            & (((back_col >> 2) & 3) == q)
            & ((back_col & 3) == (back_row & 3))
        )
        sel_back[q] = jnp.where(hit, 1.0, 0.0).astype(BF16)
    dgn[...] = jnp.zeros_like(dgn)

    for copy in misc_copies():
        copy.wait()
    place = lax.broadcasted_iota(jnp.int32, (slots, tokens), 0)
    for s in range(2):
        table = rt[s]
        for k in range(2):
            hit = place == table[k : k + 1].astype(jnp.int32)
            pk[s, k] = jnp.where(hit, 1.0, 0.0).astype(BF16)
        gt[s] = jnp.transpose(jnp.concatenate([table] * (tokens // 8), axis=0))

    @pl.when(core == 0)
    def first_input():
        ags[0, 0, 0] = bnd[0].reshape(nx, rows, features)
        ags[1, 1, 3] = bx[...].reshape(nx, rows, features)

    @pl.when(core == 1)
    def second_input():
        ags[0, 0, 0] = bx[...].reshape(nx, rows, features)
        ags[1, 1, 3] = bnd[1].reshape(nx, rows, features)

    cur[...] = ags[0, 0, 0, mx].astype(F32)
    weight_forward(0)
    weight_ready(0)
    for s in range(2):
        turned = jnp.transpose(wg[s].astype(F32))
        gn[s] = turned[:8]

    lane = lax.broadcasted_iota(jnp.int32, (1, wide_features), 1)
    head_masks = [
        jnp.where((lane >= h * HEAD_DIM) & (lane < (h + 1) * HEAD_DIM), 1.0, 0.0).astype(BF16)
        for h in range(heads)
    ]

    def per_head(values):
        return [values * mask for mask in head_masks]

    def norm_parts(stream):
        center = stream - jnp.mean(stream, axis=-1, keepdims=True)
        scale = lax.rsqrt(jnp.mean(center * center, axis=-1, keepdims=True) + EPSILON)
        return center * scale, scale

    def norm_back(s, k, parts, grad_normed):
        normal, scale = parts
        gain_rows = jnp.sum(grad_normed * normal, axis=0, keepdims=True)
        if k == 0:

            @pl.when(s == 1)
            def not_sent_yet():
                dgn[s, k : k + 1, :] = gain_rows

        else:
            dgn[s, k : k + 1, :] = gain_rows
        pulled = grad_normed * gn[s][k : k + 1]
        return scale * (
            pulled
            - jnp.mean(pulled, axis=-1, keepdims=True)
            - normal * jnp.mean(pulled * normal, axis=-1, keepdims=True)
        )

    some = pl.ds(0, nx - 1)

    def all_rows(s, way, k, own_rows, meanwhile=None):
        ags[s, way, k, mx] = own_rows.astype(BF16)
        for step in x_steps:
            remote(
                ags.at[s, way, k, mx],
                ags.at[s, way, k, mx],
                ag_send.at[s, way, k],
                ag_recv.at[s, way, k],
                tensor=x_peer(step),
            ).start()
        if meanwhile is not None:
            meanwhile()
        wait_for(ags.at[s, way, k, some], ag_recv.at[s, way, k])
        return ags[s, way, k].reshape(tokens, features)

    def sum_start(s, way, k, partial_rows):
        rs_out[s, way, k] = partial_rows.astype(BF16).reshape(nx, rows, features)
        for step in x_steps:
            peer = x_peer(step)
            remote(
                rs_out.at[s, way, k, peer],
                rs_in.at[s, way, k, mx],
                rs_send.at[s, way, k],
                rs_recv.at[s, way, k],
                tensor=peer,
            ).start()

    def sum_end(s, way, k):
        wait_for(rs_in.at[s, way, k, some], rs_recv.at[s, way, k])
        total = rs_out[s, way, k, mx].astype(F32)
        for step in range(1, nx):
            total = total + rs_in[s, way, k, x_peer(step)].astype(F32)
        return total

    def slots_start(s, which, values):
        main = values[: nd * MAIN]
        extra = values[nd * MAIN :]
        folded = None
        for q in range(quarters):
            columns = slice(256 * q, 256 * (q + 1))
            a2_out[:, 16 * q : 16 * (q + 1), :] = main[:, columns].reshape(nd, 16, 256)
            term = nn(sel[q], extra[:, columns])
            folded = term if folded is None else folded + term
        a2_out[:, 16 * quarters :, :] = folded.astype(BF16).reshape(nd, 16, 256)

        def push(step):
            peer = d_peer(far_first(step))
            remote(
                a2_out.at[peer],
                a2_in.at[s, which, md],
                a2_send.at[0],
                a2_recv.at[s, which],
                dp=peer,
            ).start()

        each_step(push)
        a2_in[s, which, md] = a2_out[md]

    def slots_end(s, which):
        wait_for(a2_in.at[s, which, pl.ds(0, nd - 1)], a2_recv.at[s, which])
        mains = []
        extra = []
        folded = a2_in[s, which, :, 16 * quarters :, :].reshape(nd * 16, 256)
        for q in range(quarters):
            block = a2_in[s, which, :, 16 * q : 16 * (q + 1), :]
            mains.append(block.reshape(nd * 16, 256))
            extra.append(nn(sel_back[q], folded).astype(BF16))
        return jnp.concatenate(
            [jnp.concatenate(mains, axis=1), jnp.concatenate(extra, axis=1)], axis=0
        )

    def slots_sent():
        wait_for(a2_out.at[pl.ds(0, nd - 1)], a2_send.at[0])

    def dback_start(s, grad_rows):
        wide = grad_rows.astype(F32)
        gates = gt[s]
        dback = nn(pk[s, 0], (wide * gates[:, 2:3]).astype(BF16)) + nn(
            pk[s, 1], (wide * gates[:, 3:4]).astype(BF16)
        )
        slots_start(s, 2, dback.astype(BF16))

    def attend(s, j, k):
        stream = cur[...]
        hs[s, k] = stream
        normal, unused = norm_parts(stream)
        if j == 0:

            @pl.when(s != 0)
            def fetch():
                all_rows(s, 0, k, normal * gn[s][k : k + 1])

            normed = ags[s, 0, k].reshape(tokens, features)
        else:
            normed = all_rows(s, 0, k, normal * gn[s][k : k + 1])

        @pl.when(core != s)
        def weights():
            weight_ready(1 + 2 * j)

        projected = nn(normed, wa[s, j])
        query, key, value = [
            projected[:, c * wide_features : (c + 1) * wide_features].astype(BF16)
            for c in range(1, 4)
        ]
        proj[s, j, 0] = query
        proj[s, j, 1] = key
        proj[s, j, 2] = value
        logits = nt(jnp.concatenate(per_head(query), axis=0), key) * (HEAD_DIM**-0.5)
        exponent = jnp.exp(logits - jnp.max(logits, axis=-1, keepdims=True))
        probs = exponent / jnp.sum(exponent, axis=-1, keepdims=True)
        prb[s, j] = probs
        low = probs.astype(BF16)
        mixed = None
        for h, part in enumerate(per_head(value)):
            term = nn(low[h * tokens : (h + 1) * tokens], part)
            mixed = term if mixed is None else mixed + term
        mixed = mixed.astype(BF16)
        mix[s, j] = mixed
        sum_start(s, 0, k, nt(mixed, wa[s, j, :, :wide_features]))

        if j == 1:

            @pl.when((s == 0) & (core == 1))
            def share():
                share_weight(3)

            @pl.when(s == 1)
            def early_end():
                slots_sent()

        cur[...] = stream + sum_end(s, 0, k)

    def feed(s):
        stream = cur[...]
        hs[s, 1] = stream
        normal, unused = norm_parts(stream)

        def meanwhile():
            @pl.when((s == 0) & (core == 0))
            def onward():
                weight_forward(2)

        normed = all_rows(s, 0, 1, normal * gn[s][1:2], meanwhile)

        @pl.when(core != s)
        def weights():
            weight_ready(2)

        pre = nn(normed, wm[s, 0])
        phi = normal_cdf(pre)
        active = (pre * phi).astype(BF16)
        sum_start(s, 0, 1, nt(active, wm[s, 1]))
        act[s] = active
        dgm[s] = gelu_slope(pre, phi)

        @pl.when((s == 0) & (core == 0))
        def onward():
            weight_forward(3)

        @pl.when((s == 0) & (core == 1))
        def share():
            share_weight(1)
            share_weight(2)

        @pl.when(s == 1)
        def early():
            slots_sent()
            dback_start(s, ags[1, 1, 3].reshape(tokens, features))

        cur[...] = stream + sum_end(s, 0, 1)

    def experts(s):
        stream = cur[...]
        hs[s, 3] = stream
        normal, unused = norm_parts(stream)
        normed = all_rows(s, 0, 3, normal * gn[s][3:4])
        slots_start(s, 0, nn(pk[s, 0] + pk[s, 1], normed).astype(BF16))

        @pl.when(s == 0)
        def weights():
            for copy in expert_copies() + expert_own():
                copy.wait()

        sent = slots_end(s, 0)
        pre = nn(sent, we[s, 0])
        phi = normal_cdf(pre)
        active = (pre * phi).astype(BF16)
        partial_rows = nn(active, we[s, 1]).astype(BF16)
        slots_sent()
        slots_start(s, 1, partial_rows)
        arr[s] = sent
        ace[s] = active
        dge[s] = gelu_slope(pre, phi)

    def experts_start(s):
        back = slots_end(s, 1)
        gates = gt[s]
        partial_rows = tn(pk[s, 0], back) * gates[:, 2:3] + tn(pk[s, 1], back) * gates[:, 3:4]
        sum_start(s, 0, 3, partial_rows)

    def experts_end(s):
        return hs[s, 3] + sum_end(s, 0, 3)

    def forward(s, carry):
        cur[...] = cur[...].astype(BF16).astype(F32)
        attend(s, 0, 0)
        feed(s)
        attend(s, 1, 2)
        experts(s)

        @pl.when(s == 0)
        def to_the_next():
            @pl.when(core == 1)
            def onward():
                for which in range(1, 4):
                    weight_forward(which)

            experts_start(s)
            cur[...] = experts_end(s)

        return carry

    def result_copies(buffer, target, start):
        slot = core * nx + mx

        @pl.when(core == target)
        def near():
            copy = local(buffer, res.at[slot], res_own.at[0])
            copy.start() if start else copy.wait()

        @pl.when(core != target)
        def far():
            copy = remote(
                buffer,
                res.at[slot],
                res_send.at[1],
                res_recv.at[0],
                pipe=target,
            )
            copy.start() if start else copy.wait_send()

        for step in range(1, nx):
            copy = remote(
                buffer,
                res.at[slot],
                res_send.at[1 + step],
                res_recv.at[0],
                pipe=target,
                tensor=x_peer(step),
            )
            copy.start() if start else copy.wait_send()

    @pl.when(core == 0)
    def first_weights():
        weight_forward(1)

    for copy in expert_copies() + expert_own():
        copy.start()
    given = ags[0, 0, 0].reshape(tokens, features).astype(F32)
    normal, unused = norm_parts(given)
    xh[...] = normal
    ags[0, 0, 0] = (normal * gn[0][0:1]).astype(BF16).reshape(nx, rows, features)
    lax.fori_loop(0, 2, forward, 0)

    staged = (ga.at[0], gm, ga.at[1])
    partner = (pa.at[0], pm, pa.at[1])
    landing = (ra.at[0], rm, ra.at[1])

    def some_rows(which, part):
        return staged[which].at[:, part] if which == 1 else staged[which].at[part]

    def chunk(which, owner):
        return some_rows(which, pl.ds(owner * shard_rows, shard_rows))

    def staged_wait(which, section):
        @pl.when(core == section)
        def owned():
            wait_for(some_rows(which, all_but_one), ch_send.at[which])
            local(chunk(which, md), landing[which].at[md], ch_own.at[which]).wait()

        @pl.when(core != section)
        def lent():
            wait_for(staged[which], pg_send.at[which])

    def lend(which, section):
        @pl.when(core != section)
        def lent():
            remote(
                staged[which],
                partner[which],
                pg_send.at[which],
                pg_recv.at[which],
                pipe=other,
            ).start()

    def combine(which, section):
        @pl.when(core == section)
        def owned():
            wait_for(partner[which], pg_recv.at[which])
            staged[which][...] = (
                staged[which][...].astype(F32) + partner[which][...].astype(F32)
            ).astype(BF16)

            def push(step):
                peer = d_peer(step)
                remote(
                    chunk(which, peer),
                    landing[which].at[md],
                    ch_send.at[which],
                    ch_recv.at[which],
                    dp=peer,
                ).start()

            each_step(push)
            local(chunk(which, md), landing[which].at[md], ch_own.at[which]).start()

    def gains_start():
        place_here = core * nx + mx
        for section in range(2):

            @pl.when(core == section)
            def near():
                gx[place_here] = dgn[section]

            @pl.when(core != section)
            def far():
                remote(
                    dgn.at[section],
                    gx.at[place_here],
                    gx_send.at[section, 0],
                    gx_recv.at[0],
                    pipe=section,
                ).start()

            for step in range(1, nx):
                remote(
                    dgn.at[section],
                    gx.at[place_here],
                    gx_send.at[section, step],
                    gx_recv.at[0],
                    pipe=section,
                    tensor=x_peer(step),
                ).start()

    def gains_push():
        wait_for(gx.at[pl.ds(0, 2 * nx - 1)], gx_recv.at[0])
        gains_total = gx[0]
        for source in range(1, 2 * nx):
            gains_total = gains_total + gx[source]
        gs[...] = gains_total

        def push_gains(step):
            remote(gs, rg.at[md], rg_send.at[0], rg_recv.at[0], dp=d_peer(step)).start()

        each_step(push_gains)
        local(gs, rg.at[md], rg_own.at[0]).start()

    def experts_back(s):
        grad = cur[...]

        @pl.when(s == 0)
        def later():
            wide = all_rows(s, 1, 3, grad, slots_sent)
            dback_start(s, wide)
            combine(0, 1)

        dback = slots_end(s, 2)
        dpre = (nt(dback, we[s, 1]) * dge[s]).astype(BF16)
        dsent = nt(dpre, we[s, 0]).astype(BF16)
        slots_sent()
        slots_start(s, 3, dsent)

        @pl.when(s == 1)
        def last_result_start():
            experts_start(s)

        eg[0] = tn(arr[s], dpre).astype(BF16)
        eg[1] = tn(ace[s], dback).astype(BF16)

        @pl.when(core == s)
        def keep():
            local(eg.at[0], ei_own, e_own.at[0]).start()
            local(eg.at[1], eo_own, e_own.at[1]).start()

        @pl.when(core != s)
        def give():
            remote(eg.at[0], ei_far, e_send.at[0], e_recv.at[0], pipe=other).start()
            remote(eg.at[1], eo_far, e_send.at[1], e_recv.at[1], pipe=other).start()

        @pl.when(s == 1)
        def last_result_end():
            hout[...] = experts_end(s)
            result_copies(hout, 1, True)

        parts = norm_parts(hs[s, 3])
        dsent = slots_end(s, 3)
        sum_start(s, 1, 3, tn(pk[s, 0] + pk[s, 1], dsent))
        cur[...] = grad + norm_back(s, 3, parts, sum_end(s, 1, 3))

    def attend_back(s, j, k):
        grad = cur[...]
        dz = all_rows(s, 1, k, grad, (lambda: combine(1, s)) if j == 0 else None)
        dmixed = nn(dz, wa[s, j, :, :wide_features]).astype(BF16)
        query, key, value = [proj[s, j, c] for c in range(3)]
        probs = prb[s, j]
        dmixed_heads = jnp.concatenate(per_head(dmixed), axis=0)
        dprobs = nt(dmixed_heads, value)
        dscores = probs * (dprobs - jnp.sum(probs * dprobs, axis=-1, keepdims=True))
        dscores = dscores.astype(BF16)
        dvalue = tn(probs.astype(BF16), dmixed_heads)
        dkey = tn(dscores, jnp.concatenate(per_head(query), axis=0)) * (HEAD_DIM**-0.5)
        dquery = None
        for h, part in enumerate(per_head(key)):
            term = nn(dscores[h * tokens : (h + 1) * tokens], part)
            dquery = term if dquery is None else dquery + term
        dquery = dquery * (HEAD_DIM**-0.5)
        dproj = [d.astype(BF16) for d in (dquery, dkey, dvalue)]
        placed = None
        for c in range(3):
            term = nn(dproj[c], put[1 + c])
            placed = term if placed is None else placed + term
        placed = placed.astype(BF16)
        partial_rows = nt(placed, wa[s, j])

        def weight_grads():
            normed = ags[s, 0, k].reshape(tokens, features)
            mixed = nn(mix[s, j], put[0]).astype(BF16)
            ga[j] = tn(
                jnp.concatenate([normed, dz], axis=0), jnp.concatenate([placed, mixed], axis=0)
            ).astype(BF16)
            lend(2 * j, s)

        if j == 0:

            @pl.when(s == 0)
            def last_of_all():
                dgn[0, 0:1, :] = jnp.sum(partial_rows * xh[...], axis=0, keepdims=True)
                gains_start()
                staged_wait(0, 1)
                weight_grads()

            sum_start(s, 1, k, partial_rows)

            @pl.when(s == 1)
            def not_last():
                weight_grads()

            @pl.when(s == 0)
            def last_onward():
                gains_push()
                combine(0, 0)

        else:
            sum_start(s, 1, k, partial_rows)

            @pl.when(s == 0)
            def free():
                staged_wait(2, 1)

            weight_grads()

        parts = norm_parts(hs[s, k])
        cur[...] = grad + norm_back(s, k, parts, sum_end(s, 1, k))

    def feed_back(s):
        grad = cur[...]
        dout = all_rows(s, 1, 1, grad, lambda: combine(2, s))
        dpre = (nn(dout, wm[s, 1]) * dgm[s]).astype(BF16)
        sum_start(s, 1, 1, nt(dpre, wm[s, 0]))

        @pl.when(s == 0)
        def free():
            staged_wait(1, 1)

        normed = ags[s, 0, 1].reshape(tokens, features)
        gm[0] = tn(normed, dpre).astype(BF16)
        gm[1] = tn(dout, act[s]).astype(BF16)
        lend(1, s)
        parts = norm_parts(hs[s, 1])
        cur[...] = grad + norm_back(s, 1, parts, sum_end(s, 1, 1))

    def expert_grads_wait(s):
        @pl.when(core == s)
        def keep():
            local(eg.at[0], ei_own, e_own.at[0]).wait()
            local(eg.at[1], eo_own, e_own.at[1]).wait()

        @pl.when(core != s)
        def give():
            wait_for(eg.at[0], e_send.at[0])
            wait_for(eg.at[1], e_send.at[1])

    def backward(turn, carry):
        s = 1 - turn
        cur[...] = cur[...].astype(BF16).astype(F32)
        experts_back(s)
        attend_back(s, 1, 2)
        feed_back(s)
        attend_back(s, 0, 0)
        expert_grads_wait(s)
        return carry

    cur[...] = ags[1, 1, 3, mx].astype(F32)
    lax.fori_loop(0, 2, backward, 0)
    gout[...] = cur[...]
    result_copies(hout, 1, False)
    result_copies(gout, 0, True)

    slots_sent()
    for s in range(2):
        for way in range(2):
            for k in range(4):
                wait_for(rs_out.at[s, way, k, some], rs_send.at[s, way, k])
                if (s, way, k) not in ((0, 0, 0), (1, 1, 3)):
                    wait_for(ags.at[s, way, k, some], ag_send.at[s, way, k])
    for section in range(2):

        @pl.when(core != section)
        def far_end():
            wait_for(dgn.at[section], gx_send.at[section, 0])

        for step in range(1, nx):
            wait_for(dgn.at[section], gx_send.at[section, step])
    for which in range(4):
        wait_for(whole_part(which, 0), wf_send.at[which])
        wait_for(arrived_part(which), w_send.at[which])
    result_copies(gout, 0, False)
    wait_for(res.at[pl.ds(0, 2 * nx - 1)], res_recv.at[0])
    def over_sources(parts):
        total = parts[0].astype(F32)
        for source in range(1, nd):
            total = total + parts[source].astype(F32)
        return total

    def landed(which):
        staged_wait(which, 0)
        wait_for(landing[which].at[pl.ds(0, nd - 1)], ch_recv.at[which])

    landed(2)
    dense_sum[1] = over_sources(ra[1])
    landed(1)
    for c in range(2):
        feed_sum[c] = over_sources([rm[source, c] for source in range(nd)])
    wait_for(ei_far, e_recv.at[0])
    wait_for(eo_far, e_recv.at[1])
    wait_for(rg.at[pl.ds(0, nd - 1)], rg_recv.at[0])
    wait_for(rg.at[pl.ds(0, nd - 1)], rg_send.at[0])
    local(gs, rg.at[md], rg_own.at[0]).wait()
    gains_sum[...] = over_sources(rg)
    landed(0)
    dense_sum[0] = over_sources(ra[0])


def shards(
    nx,
    nd,
    boundary,
    norm_gains,
    attn_qkv,
    attn_out,
    mlp_in,
    mlp_out,
    expert_in,
    expert_out,
    expert_ids,
    expert_slots,
    gate_weights,
):
    tokens, features = boundary.shape[3:]
    rows = tokens // nx
    shard_rows = features // nd
    wide = attn_qkv.shape[4]
    units = mlp_in.shape[2]
    hidden = expert_in.shape[3]
    slots = nd * CAP
    quarters = features // 256
    slab = 16 * quarters + 16
    heads = wide // HEAD_DIM

    vmem = pl.BlockSpec(memory_space=pltpu.VMEM)
    hbm = pl.BlockSpec(memory_space=pl.ANY)
    dma = pltpu.SemaphoreType.DMA
    scratch = [
        pltpu.VMEM((2, nd, shard_rows, 4 * wide), BF16),
        pltpu.VMEM((nd, 2, shard_rows, units), BF16),
        pltpu.VMEM((nd, 8, features), F32),
        pltpu.VMEM((MICRO, 8, tokens), F32),
        pltpu.VMEM((shard_rows, 128), BF16),
        pltpu.VMEM((2, shard_rows, 4 * wide), BF16),
        pltpu.VMEM((2, shard_rows, units), BF16),
        pltpu.VMEM((4, wide, 4 * wide), BF16),
        pltpu.VMEM((tokens, features), F32),
        pltpu.VMEM((2, 2, features, 4 * wide), BF16),
        pltpu.VMEM((2, 2, features, units), BF16),
        pltpu.VMEM((2, 2, features, hidden), BF16),
        pltpu.VMEM((2, features, 128), BF16),
        pltpu.VMEM((2, 8, features), F32),
        pltpu.VMEM((2, 8, tokens), F32),
        pltpu.VMEM((2, tokens, tokens), F32),
        pltpu.VMEM((tokens, features), BF16),
        pltpu.VMEM((quarters, nd * 16, nd * (CAP - MAIN)), BF16),
        pltpu.VMEM((quarters, nd * (CAP - MAIN), nd * 16), BF16),
        pltpu.VMEM((2, 2, slots, tokens), BF16),
        pltpu.VMEM((2, 4, rows, features), F32),
        pltpu.VMEM((2, 2, 4, nx, rows, features), BF16),
        pltpu.VMEM((2, 2, 4, nx, rows, features), BF16),
        pltpu.VMEM((2, 2, 4, nx, rows, features), BF16),
        pltpu.VMEM((nd, slab, 256), BF16),
        pltpu.VMEM((2, 4, nd, slab, 256), BF16),
        pltpu.VMEM((2, 2, 3, tokens, wide), BF16),
        pltpu.VMEM((2, 2, tokens, wide), BF16),
        pltpu.VMEM((2, 2, heads * tokens, tokens), F32),
        pltpu.VMEM((2, tokens, units), F32),
        pltpu.VMEM((2, tokens, units), BF16),
        pltpu.VMEM((2, slots, features), BF16),
        pltpu.VMEM((2, slots, hidden), F32),
        pltpu.VMEM((2, slots, hidden), BF16),
        pltpu.VMEM((2, features, 4 * wide), BF16),
        pltpu.VMEM((2, features, units), BF16),
        pltpu.VMEM((2, features, 4 * wide), BF16),
        pltpu.VMEM((2, features, units), BF16),
        pltpu.VMEM((2, features, hidden), BF16),
        pltpu.VMEM((2, 8, features), F32),
        pltpu.VMEM((2 * nx, 8, features), F32),
        pltpu.VMEM((8, features), F32),
        pltpu.VMEM((rows, features), F32),
        pltpu.VMEM((rows, features), F32),
        pltpu.VMEM((rows, features), F32),
        dma((2, 2, 4)),
        dma((2, 2, 4)),
        dma((2, 2, 4)),
        dma((2, 2, 4)),
        dma((1,)),
        dma((2, 4)),
        dma((4,)),
        dma((4,)),
        dma((4,)),
        dma((4,)),
        dma((4,)),
        dma((4,)),
        dma((4,)),
        dma((2,)),
        dma((3,)),
        dma((3,)),
        dma((3,)),
        dma((3,)),
        dma((3,)),
        dma((2,)),
        dma((2,)),
        dma((2,)),
        dma((1 + nx,)),
        dma((1,)),
        dma((1,)),
        dma((2, nx)),
        dma((1,)),
        dma((1,)),
        dma((1,)),
        dma((1,)),
    ]
    res, dense, feed, gains, ei_own, eo_own, ei_far, eo_far = pl.pallas_call(
        functools.partial(kernel, nx, nd),
        out_shape=(
            jax.ShapeDtypeStruct((2 * nx, rows, features), F32),
            jax.ShapeDtypeStruct((2, shard_rows, 4 * wide), F32),
            jax.ShapeDtypeStruct((2, shard_rows, units), F32),
            jax.ShapeDtypeStruct((8, features), F32),
            jax.ShapeDtypeStruct((features, hidden), BF16),
            jax.ShapeDtypeStruct((hidden, features), BF16),
            jax.ShapeDtypeStruct((features, hidden), BF16),
            jax.ShapeDtypeStruct((hidden, features), BF16),
        ),
        in_specs=[vmem] * 9 + [hbm] * 2,
        out_specs=(hbm,) + (vmem,) * 3 + (hbm,) * 4,
        scratch_shapes=scratch,
        compiler_params=pltpu.CompilerParams(
            collective_id=0, has_side_effects=True, vmem_limit_bytes=VMEM_LIMIT
        ),
    )(
        boundary[0, :, 0],
        jnp.swapaxes(expert_ids[0, :, 0], 1, 2),
        jnp.swapaxes(expert_slots[0, :, 0], 1, 2),
        jnp.swapaxes(gate_weights[0, :, 0], 1, 2),
        attn_qkv[0],
        jnp.swapaxes(attn_out[0], 1, 2),
        mlp_in[0],
        mlp_out[0].T,
        norm_gains[0],
        expert_in[0, 0],
        expert_out[0, 0],
    )

    gains = gains[: norm_gains.shape[1]]
    gains = lax.dynamic_slice_in_dim(gains, lax.axis_index("dp") * shard_rows, shard_rows, 1)
    qkv = dense[:, :, wide:].reshape(2, shard_rows, 3, wide)
    return (
        res.reshape(1, MICRO, 1, tokens, features),
        gains[None],
        jnp.swapaxes(qkv, 1, 2)[None],
        jnp.swapaxes(dense[:, :, :wide], 1, 2)[None],
        feed[0][None],
        feed[1].T[None],
        (ei_own.astype(F32) + ei_far.astype(F32))[None, None],
        (eo_own.astype(F32) + eo_far.astype(F32))[None, None],
    )


VMEM_LIMIT = 62 * 1024 * 1024


def solution(mesh):
    in_specs = (
        P("pipe", None, "dp", None, None),
        P("pipe", None, "dp"),
        P("pipe", None, None, "dp", "tensor"),
        P("pipe", None, "tensor", "dp"),
        P("pipe", "dp", "tensor"),
        P("pipe", "tensor", "dp"),
        P("pipe", "dp", None, "tensor"),
        P("pipe", "dp", "tensor", None),
        P("pipe", None, "dp", None, None),
        P("pipe", None, "dp", None, None),
        P("pipe", None, "dp", None, None),
    )
    out_specs = (
        P("pipe", None, "dp", None, None),
        P("pipe", None, "dp"),
        P("pipe", None, None, "dp", "tensor"),
        P("pipe", None, "tensor", "dp"),
        P("pipe", "dp", "tensor"),
        P("pipe", "tensor", "dp"),
        P("pipe", "dp", None, "tensor"),
        P("pipe", "dp", "tensor", None),
    )
    return jax.shard_map(
        functools.partial(shards, mesh.shape["tensor"], mesh.shape["dp"]),
        mesh=mesh,
        in_specs=in_specs,
        out_specs=out_specs,
        check_vma=False,
    )
```

profile of v0, /device:TPU:0, one launch (start us, length us, event | category | flops | bytes accessed | tf_op | source)
XLA Modules:
  0.0 278.7 jit_solution(9142755667740326563)
XLA Ops:
  0.6 268.9 %shard_map.170 = (f32[8,32,768]{2,1,0:T(8,128)}, f32[2,48,768]{2,1,0:T(8,128)}, f32[2,48,768]{2,1,0:T(8,128)}, f32[8,768]{1,0:T(8,128)}, bf16[768,768]{1,0:T(8,1...) custom-call(bf16[2,128,768]{2,1,0:T(8,128)(2,1)} %bitcast.47, ...), custom_call_target="tpu_custom_call" | custom-call | tf_op jit(solution)/shard_map/pallas_call | solution.py:1075
  269.6 0.0 copy-start.3
  269.6 0.0 copy-start.1
  269.6 5.1 %add_bitcast_fusion = (f32[1,1,768,768]{3,2,1,0:T(8,128)}, f32[1,1,768,768]{3,2,1,0:T(8,128)}) fusion(bf16[768,768]{1,0:T(8,128)(2,1)} %get-tuple-element.23, bf16[768,768]{1,0:T(8,128)(2,1)} %get-tuple-element.22, bf16[768,768]{1,0:T(8,128)(2,1)} %get-tuple-element.21, bf16[768,768]{1,0:T(8,128)(2,1)} %get-tuple-element.20), kind=kLoop, calls=%fused_computation | loop fusion | flops 3538944 | bytes 9437184 | tf_op jit(solution)/shard_map/broadcast_in_dim | solution.py:1118
  274.7 0.0 copy-start.2
  274.7 0.0 copy-done.3
  274.7 0.7 dynamic-slice_bitcast_fusion
  275.3 0.0 copy-done.1
  275.3 0.1 slice.16
  275.5 0.0 copy-start
  275.5 0.2 reshape.23
  275.7 0.8 copy.22
  276.4 0.0 copy-done.2
  276.4 0.7 slice_bitcast_fusion
  277.2 0.6 slice_bitcast_fusion.1
  277.8 0.0 copy-done
  277.8 0.9 copy.24
  (1 shorter events, 0.0 us)
Async XLA Ops:
  269.6 5.1 %copy-start.3 = (f32[8,768]{1,0:T(8,128)S(1)}, f32[8,768]{1,0:T(8,128)}, u32[]{:S(2)}) copy-start(f32[8,768]{1,0:T(8,128)} %get-tuple-element.17) | copy-start | bytes 73732
  269.6 5.8 %copy-start.1 = (f32[2,48,768]{2,1,0:T(8,128)S(1)}, f32[2,48,768]{2,1,0:T(8,128)}, u32[]{:S(2)}) copy-start(f32[2,48,768]{2,1,0:T(8,128)} %get-tuple-element.18) | copy-start | bytes 884740
  274.7 1.8 copy-start.2
  275.5 2.3 copy-start
where the time goes:
time: 279 us
  Pallas kernels  269 us (96%)
  other arithmetic  5.08 us (2%)
  local copies, waits for them, and re-layouts  3.99 us (1%)
    pallas_call x1, Pallas kernels, shards(): pl.pallas_call(functools.partial(kernel, nx, nd), out_shape=(jax.ShapeDty...  269 us

commit v1 on v0

--- a/solution.py
+++ b/solution.py
@@ -174,10 +174,6 @@
 
         lax.fori_loop(0, (nd - 1) // unit, some_steps, 0)
 
-    def far_first(step):
-        turned = step + nd // 2 - 1
-        return jnp.where(turned >= nd, turned - nd + 1, turned)
-
     def remote(src, dst, send, recv, **where):
         return pltpu.make_async_remote_copy(
             src_ref=src,
@@ -458,7 +454,7 @@
         a2_out[:, 16 * quarters :, :] = folded.astype(BF16).reshape(nd, 16, 256)
 
         def push(step):
-            peer = d_peer(far_first(step))
+            peer = d_peer(step)
             remote(
                 a2_out.at[peer],
                 a2_in.at[s, which, md],

time: 279 us -> 278 us (level)
  no operation moved by 1% of the time
where the time goes in v1:
time: 278 us; the launch traced here: 277 us
  Pallas kernels  268 us (96%)
  other arithmetic  5.08 us (2%)
  local copies, waits for them, and re-layouts  3.99 us (1%)
    pallas_call x1, Pallas kernels, shards(): pl.pallas_call(functools.partial(kernel, nx, nd), out_shape=(jax.ShapeDty...  268 us

profile of v1, /device:TPU:0, one launch (start us, length us, event | category | flops | bytes accessed | tf_op | source)
XLA Modules:
  0.0 277.4 jit_solution(15722310531604781471)
XLA Ops:
  0.6 267.7 %shard_map.170 = (f32[8,32,768]{2,1,0:T(8,128)}, f32[2,48,768]{2,1,0:T(8,128)}, f32[2,48,768]{2,1,0:T(8,128)}, f32[8,768]{1,0:T(8,128)}, bf16[768,768]{1,0:T(8,1...) custom-call(bf16[2,128,768]{2,1,0:T(8,128)(2,1)} %bitcast.47, ...), custom_call_target="tpu_custom_call" | custom-call | tf_op jit(solution)/shard_map/pallas_call | solution.py:1071
  268.3 0.0 copy-start.3
  268.3 0.0 copy-start.1
  268.3 5.1 %add_bitcast_fusion = (f32[1,1,768,768]{3,2,1,0:T(8,128)}, f32[1,1,768,768]{3,2,1,0:T(8,128)}) fusion(bf16[768,768]{1,0:T(8,128)(2,1)} %get-tuple-element.23, bf16[768,768]{1,0:T(8,128)(2,1)} %get-tuple-element.22, bf16[768,768]{1,0:T(8,128)(2,1)} %get-tuple-element.21, bf16[768,768]{1,0:T(8,128)(2,1)} %get-tuple-element.20), kind=kLoop, calls=%fused_computation | loop fusion | flops 3538944 | bytes 9437184 | tf_op jit(solution)/shard_map/broadcast_in_dim | solution.py:1114
  273.4 0.0 copy-start.2
  273.4 0.0 copy-done.3
  273.4 0.7 dynamic-slice_bitcast_fusion
  274.1 0.0 copy-done.1
  274.1 0.1 slice.16
  274.2 0.0 copy-start
  274.2 0.2 reshape.23
  274.4 0.8 copy.22
  275.2 0.0 copy-done.2
  275.2 0.7 slice_bitcast_fusion
  275.9 0.6 slice_bitcast_fusion.1
  276.5 0.0 copy-done
  276.5 0.9 copy.24
  (1 shorter events, 0.0 us)
Async XLA Ops:
  268.3 5.1 %copy-start.3 = (f32[8,768]{1,0:T(8,128)S(1)}, f32[8,768]{1,0:T(8,128)}, u32[]{:S(2)}) copy-start(f32[8,768]{1,0:T(8,128)} %get-tuple-element.17) | copy-start | bytes 73732
  268.3 5.8 %copy-start.1 = (f32[2,48,768]{2,1,0:T(8,128)S(1)}, f32[2,48,768]{2,1,0:T(8,128)}, u32[]{:S(2)}) copy-start(f32[2,48,768]{2,1,0:T(8,128)} %get-tuple-element.18) | copy-start | bytes 884740
  273.4 1.8 copy-start.2
  274.2 2.3 copy-start

commit v2 on v1

--- a/solution.py
+++ b/solution.py
@@ -192,13 +192,12 @@
 
     barrier = pltpu.get_barrier_semaphore()
 
-    def greet(step, carry):
+    def greet(step):
         pl.semaphore_signal(
             barrier, inc=1, device_id={"dp": d_peer(step)}, device_id_type=MESH
         )
-        return carry
-
-    lax.fori_loop(1, nd, greet, 0)
+
+    each_step(greet)
     for step in range(1, nx):
         pl.semaphore_signal(
             barrier, inc=1, device_id={"tensor": x_peer(step)}, device_id_type=MESH
@@ -485,8 +484,9 @@
     def dback_start(s, grad_rows):
         wide = grad_rows.astype(F32)
         gates = gt[s]
-        dback = nn(pk[s, 0], (wide * gates[:, 2:3]).astype(BF16)) + nn(
-            pk[s, 1], (wide * gates[:, 3:4]).astype(BF16)
+        weighted = [(wide * gates[:, c : c + 1]).astype(BF16) for c in (2, 3)]
+        dback = nn(
+            jnp.concatenate([pk[s, 0], pk[s, 1]], axis=1), jnp.concatenate(weighted, axis=0)
         )
         slots_start(s, 2, dback.astype(BF16))
 
@@ -858,8 +858,8 @@
 
             @pl.when(s == 0)
             def last_onward():
+                combine(0, 0)
                 gains_push()
-                combine(0, 0)
 
         else:
             sum_start(s, 1, k, partial_rows)

time: 278 us -> 278 us (level)
  no operation moved by 1% of the time
where the time goes in v2:
time: 278 us
  Pallas kernels  268 us (96%)
  other arithmetic  5.08 us (2%)
  local copies, waits for them, and re-layouts  3.99 us (1%)
    pallas_call x1, Pallas kernels, shards(): pl.pallas_call(functools.partial(kernel, nx, nd), out_shape=(jax.ShapeDty...  268 us

profile of v2, /device:TPU:0, one launch (start us, length us, event | category | flops | bytes accessed | tf_op | source)
XLA Modules:
  0.0 278.3 jit_solution(15964938136799871502)
XLA Ops:
  0.6 268.5 %shard_map.170 = (f32[8,32,768]{2,1,0:T(8,128)}, f32[2,48,768]{2,1,0:T(8,128)}, f32[2,48,768]{2,1,0:T(8,128)}, f32[8,768]{1,0:T(8,128)}, bf16[768,768]{1,0:T(8,1...) custom-call(bf16[2,128,768]{2,1,0:T(8,128)(2,1)} %bitcast.47, ...), custom_call_target="tpu_custom_call" | custom-call | tf_op jit(solution)/shard_map/pallas_call | solution.py:1071
  269.1 0.0 copy-start.3
  269.2 0.0 copy-start.1
  269.2 5.1 %add_bitcast_fusion = (f32[1,1,768,768]{3,2,1,0:T(8,128)}, f32[1,1,768,768]{3,2,1,0:T(8,128)}) fusion(bf16[768,768]{1,0:T(8,128)(2,1)} %get-tuple-element.23, bf16[768,768]{1,0:T(8,128)(2,1)} %get-tuple-element.22, bf16[768,768]{1,0:T(8,128)(2,1)} %get-tuple-element.21, bf16[768,768]{1,0:T(8,128)(2,1)} %get-tuple-element.20), kind=kLoop, calls=%fused_computation | loop fusion | flops 3538944 | bytes 9437184 | tf_op jit(solution)/shard_map/broadcast_in_dim | solution.py:1114
  274.2 0.0 copy-start.2
  274.2 0.0 copy-done.3
  274.3 0.7 dynamic-slice_bitcast_fusion
  274.9 0.0 copy-done.1
  274.9 0.1 slice.16
  275.0 0.0 copy-start
  275.1 0.2 reshape.23
  275.2 0.8 copy.22
  276.0 0.0 copy-done.2
  276.0 0.7 slice_bitcast_fusion
  276.7 0.6 slice_bitcast_fusion.1
  277.4 0.0 copy-done
  277.4 0.9 copy.24
  (1 shorter events, 0.0 us)
Async XLA Ops:
  269.1 5.1 %copy-start.3 = (f32[8,768]{1,0:T(8,128)S(1)}, f32[8,768]{1,0:T(8,128)}, u32[]{:S(2)}) copy-start(f32[8,768]{1,0:T(8,128)} %get-tuple-element.17) | copy-start | bytes 73732
  269.2 5.8 %copy-start.1 = (f32[2,48,768]{2,1,0:T(8,128)S(1)}, f32[2,48,768]{2,1,0:T(8,128)}, u32[]{:S(2)}) copy-start(f32[2,48,768]{2,1,0:T(8,128)} %get-tuple-element.18) | copy-start | bytes 884740
  274.2 1.8 copy-start.2
  275.0 2.3 copy-start
